TPU v7x, 512 devices: a whole 4x4x16 slice. The times are simulated.
512 devices in a mesh: frame: 32 (over y, x, core), seq: 16 (over z).
Axes of the slice: x: 4, y: 4, z: 16, core: 2. Of those that a mesh axis runs over, the one named last changes fastest.
Arguments:
- queries: bfloat16 [32, 2048, 2048], P('frame', 'seq'), may hold values from -23 to 23
- key_proj: bfloat16 [32, 2048, 2048], P('frame', 'seq'), may hold values from -7 to 7
- values: bfloat16 [32, 2048, 2048], P('frame', 'seq'), may hold values from -6 to 6
- back_count: int32 [32], P('frame'), may hold values from 0 to 1
- ahead_count: int32 [32], P('frame'), may hold values from 0 to 1
- timestep: int32 [32], P('frame'), may hold values from 1 to 50
- latent: float32 [32, 2048, 64], P('frame', 'seq'), may hold values from -6 to 6
- noise_frame: float32 [2048, 64], P('seq'), may hold values from -6 to 6
- w_final: bfloat16 [2048, 64], replicated, may hold values from -0.5 to 0.5
Outputs:
- velocity: float32 [32, 2048, 64], P('frame', 'seq')
- new_queue: float32 [32, 2048, 64], P('frame', 'seq')
All inputs are finite; a program needn't handle non-finite values.
Results may differ from a plain program's by a relative error of at most 0.0041.
Values may be sent and summed in bfloat16 or wider, within the bound.
A program may use at most 64 MiB of HBM per device.

v0:
```python
import functools
import math

import jax
import jax.numpy as jnp
from jax import lax
from jax.experimental import pallas as pl
from jax.experimental.pallas import tpu as pltpu
from jax.sharding import PartitionSpec as P

HD = 128
TOKS = 128
LAT = 64
STEPS = 50
SHIFT = 7.0
RATE = HD ** (-0.5) * math.log2(math.e)
F32, BF16 = jnp.float32, jnp.bfloat16
CHUNK = 256
PAIR = 2 * TOKS
SUMS = 16
GROUPS = 4
HOPS = ()


def sigma_of(index):
    share = index / STEPS
    return SHIFT * share / (1.0 + (SHIFT - 1.0) * share)


def kernel(
    ns, nf, back_hbm, ahead_hbm, time_hbm, q_hbm, k_hbm, v_hbm, w_hbm, latent_hbm, noise_hbm,
    vel_ref, new_ref,
    back_ref, ahead_ref, time_ref, v_ref, w_ref, latent_ref, noise_ref, keys, vals, vsend, weighted, qbuf, osend, obuf, hsend, hbuf, mine, theirs, s0, s1,
    own_sem, k_out, v_out, q_out, o_out, h_out, f_out, m_sems, k_in, v_in, q_in, o_in, h_in, f_in,
):
    place, here = lax.axis_index("frame"), lax.axis_index("seq")
    after, before = lax.rem(place + 1, nf), lax.rem(place + nf - 1, nf)
    half = ns // 2
    per = ns // GROUPS
    toks = ns * TOKS

    def offset(j):
        return jnp.where(j == 0, 0, jnp.where(j % 2 == 0, half - j // 2, (j - 1) // 2 - half))

    def peer(j, sign):
        return lax.rem(here + sign * offset(j) + ns, ns)

    def rows(j, count=1):
        return pl.ds(pl.multiple_of(j * TOKS, TOKS), count * TOKS)

    def lats(j, count=1):
        return pl.ds(pl.multiple_of(j * LAT, LAT), count * LAT)

    def to_seq(src, dst, send, recv, z):
        return pltpu.make_async_remote_copy(
            src_ref=src, dst_ref=dst, send_sem=send, recv_sem=recv,
            device_id={"seq": z}, device_id_type=pl.DeviceIdType.MESH)

    def to_frame(src, dst, send, recv, f):
        return pltpu.make_async_remote_copy(
            src_ref=src, dst_ref=dst, send_sem=send, recv_sem=recv,
            device_id={"frame": f}, device_id_type=pl.DeviceIdType.MESH)

    barrier = pltpu.get_barrier_semaphore()

    def greet(j, _):
        pl.semaphore_signal(barrier, inc=1, device_id={"seq": peer(j, 1)},
                            device_id_type=pl.DeviceIdType.MESH)
        return 0

    lax.fori_loop(1, ns, greet, 0)
    for f in (after, before):
        pl.semaphore_signal(barrier, inc=1, device_id={"frame": f},
                            device_id_type=pl.DeviceIdType.MESH)

    def columns(h):
        return pl.ds(pl.multiple_of(h * HD, HD), HD)

    own_v = pltpu.make_async_copy(v_hbm.at[0], v_ref, own_sem.at[2])
    own_w = pltpu.make_async_copy(w_hbm, w_ref, own_sem.at[3])
    own_latent = pltpu.make_async_copy(latent_hbm.at[0], latent_ref, own_sem.at[4])
    own_noise = pltpu.make_async_copy(noise_hbm, noise_ref, own_sem.at[5])
    scalars = [
        pltpu.make_async_copy(src, dst, own_sem.at[6 + i])
        for i, (src, dst) in enumerate(((back_hbm, back_ref), (ahead_hbm, ahead_ref), (time_hbm, time_ref)))
    ]
    own_q = pltpu.make_async_copy(q_hbm.at[0, :, columns(here)], qbuf.at[rows(0)], own_sem.at[0])
    own_k = pltpu.make_async_copy(k_hbm.at[0, :, columns(here)], keys.at[rows(0)], own_sem.at[1])
    for copy in (own_v, own_w, own_k, own_q, own_latent, own_noise, *scalars):
        copy.start()

    pl.semaphore_wait(barrier, ns + 1)

    def send_k(j, _):
        z = peer(j, 1)
        to_seq(k_hbm.at[0, :, columns(z)], keys.at[rows(j)], k_out, k_in.at[j], z).start()
        return 0

    def send_v(j, _):
        z = peer(j, 1)
        to_seq(vsend.at[lats(z)], vals.at[lats(j)], v_out, v_in.at[j], z).start()
        return 0

    def send_q(j, _):
        z = peer(j, 1)
        to_seq(q_hbm.at[0, :, columns(z)], qbuf.at[rows(j)], q_out, q_in.at[j], z).start()
        return 0

    lax.fori_loop(1, per, send_k, 0)
    own_v.wait()
    own_w.wait()
    for h in range(ns):
        part = lax.dot_general(w_ref[:, h * HD:(h + 1) * HD], v_ref[:, h * HD:(h + 1) * HD],
                               (((1,), (1,)), ((), ())), preferred_element_type=F32)
        vsend[h * LAT:(h + 1) * LAT, :] = part.astype(BF16)

    lax.fori_loop(1, per, send_v, 0)
    lax.fori_loop(per, ns, send_k, 0)
    lax.fori_loop(per, ns, send_v, 0)
    lax.fori_loop(1, ns, send_q, 0)
    vals[0:LAT, :] = vsend[lats(here), :]
    own_k.wait()
    own_q.wait()
    own_latent.wait()
    own_noise.wait()
    for copy in scalars:
        copy.wait()

    def arrived(j, _):
        to_seq(keys.at[rows(j)], keys.at[rows(j)], k_out, k_in.at[j], here).wait_recv()
        to_seq(vals.at[lats(j)], vals.at[lats(j)], v_out, v_in.at[j], here).wait_recv()
        return 0

    def forwards(g, side):
        f = (after, before)[side]
        slot = 1 + side
        return (
            to_frame(keys.at[rows(g * per, per)], keys.at[rows(slot * ns + g * per, per)],
                     f_out.at[2 * side], f_in.at[2 * side, g], f),
            to_frame(vals.at[lats(g * per, per)], vals.at[lats(slot * ns + g * per, per)],
                     f_out.at[2 * side + 1], f_in.at[2 * side + 1, g], f),
        )

    for g in range(GROUPS):
        lax.fori_loop(max(1, g * per), (g + 1) * per, arrived, 0)
        for side in range(2):
            for copy in forwards(g, side):
                copy.start()

    level = jnp.full((8, TOKS), time_ref[0], jnp.int32).astype(F32)
    step_size = (sigma_of(level - 1.0) - sigma_of(level))[0:1, :]
    latent_t = latent_ref[...]

    weighted[LAT:, 0:toks] = jnp.ones((SUMS, toks), BF16)
    for j in range(ns):
        weighted[0:LAT, j * TOKS:(j + 1) * TOKS] = vals[j * LAT:(j + 1) * LAT, :]

    has = (
        jnp.where(jnp.logical_and(back_ref[0] >= 1, place >= 1), 1.0, 0.0),
        jnp.where(jnp.logical_and(ahead_ref[0] >= 1, place <= nf - 2), 1.0, 0.0),
    )
    for side in range(2):
        slot = 1 + side
        for g in range(GROUPS):
            for copy in forwards(g, side):
                copy.wait_recv()
        yes = jnp.full((TOKS, TOKS), has[side], F32)
        no = (1.0 - yes).astype(BF16)
        yes = yes.astype(BF16)
        weighted[LAT:, slot * toks:(slot + 1) * toks] = jnp.full((SUMS, toks), has[side], F32).astype(BF16)
        for j in range(ns):
            k = slot * ns + j
            keys[k * TOKS:(k + 1) * TOKS, :] = (
                keys[k * TOKS:(k + 1) * TOKS, :] * yes + keys[j * TOKS:(j + 1) * TOKS, :] * no)
            weighted[0:LAT, k * TOKS:(k + 1) * TOKS] = vals[k * LAT:(k + 1) * LAT, :] * yes[0:LAT]

    chunks = 3 * toks // CHUNK
    blocks = ns // 2

    def hops(d, i):
        return d in HOPS and d <= half - 1 + i

    def gets(d, i):
        return hops(d + 1, i)

    def wait_q(b):
        for j in (2 * b, 2 * b + 1):
            if not isinstance(j, int) or j > 0:
                to_seq(qbuf.at[rows(j)], qbuf.at[rows(j)], q_out, q_in.at[j], here).wait_recv()
        return qbuf[pl.ds(pl.multiple_of(b * PAIR, PAIR), PAIR), :]

    def score(q, c, held, top):
        s = lax.dot_general(keys[c * CHUNK:(c + 1) * CHUNK, :], q, (((1,), (1,)), ((), ())),
                            preferred_element_type=F32)
        held[c * CHUNK:(c + 1) * CHUNK, :] = s
        t = jnp.max(s.reshape(CHUNK // 8, 8, PAIR), axis=0)
        return t if top is None else jnp.maximum(top, t)

    def gather(m, c, held, acc):
        p = jnp.exp2(held[c * CHUNK:(c + 1) * CHUNK, :] * RATE - m).astype(BF16)
        r = jnp.dot(weighted[:, c * CHUNK:(c + 1) * CHUNK], p, preferred_element_type=F32)
        return r if acc is None else acc + r

    def step_on(j, i):
        z = lax.rem(here + (1 if i else ns - 1), ns)
        return to_seq(hsend.at[lats(j)], hbuf.at[lats(j + 2)], h_out.at[j], h_in.at[j + 2], z)

    def straight(j):
        return to_seq(osend.at[lats(j)], obuf.at[lats(j)], o_out.at[j], o_in.at[j], peer(j, -1))

    def finish(b, acc):
        out = acc[0:LAT] / acc[LAT:LAT + 1]
        for i in range(2):
            j = 2 * b + i
            mine_now = out[:, i * TOKS:(i + 1) * TOKS]
            if isinstance(b, int):
                if gets(half - b, i):
                    step_on(j - 2, i).wait_recv()
                    mine_now = mine_now + hbuf[lats(j), :]
                if hops(half - b, i):
                    hsend[lats(j), :] = mine_now
                    step_on(j, i).start()
                else:
                    osend[lats(j), :] = mine_now.astype(BF16)
                    straight(j).start()
            else:
                given, stepped, own = (
                    functools.reduce(jnp.logical_or, [b == half - d for d in range(1, half + 1) if test(d, i)], False)
                    for test in (gets, hops, lambda d, i: d == half and i == 0))
                hsend[lats(j), :] = mine_now

                @pl.when(given)
                def _():
                    step_on(j - 2, i).wait_recv()
                    hsend[lats(j), :] = hsend[lats(j), :] + hbuf[lats(j), :]

                @pl.when(stepped)
                def _():
                    step_on(j, i).start()

                @pl.when(jnp.logical_not(jnp.logical_or(stepped, own)))
                def _():
                    osend[lats(j), :] = hsend[lats(j), :].astype(BF16)
                    straight(j).start()

    def peak(top):
        return jnp.max(top, axis=0, keepdims=True) * RATE

    def both(b_next, held_next, b, m, held):
        q = wait_q(b_next)
        top = acc = None
        for c in range(chunks):
            top = score(q, c, held_next, top)
            acc = gather(m, c, held, acc)
        finish(b, acc)
        return peak(top)

    q = wait_q(0)
    top = None
    for c in range(chunks):
        top = score(q, c, s0, top)
    m = peak(top)

    def two(i, m):
        m = both(2 * i + 1, s1, 2 * i, m, s0)
        return both(2 * i + 2, s0, 2 * i + 1, m, s1)

    m = lax.fori_loop(0, blocks // 2 - 1, two, m)
    m = both(blocks - 1, s1, blocks - 2, m, s0)
    acc = None
    for c in range(chunks):
        acc = gather(m, c, s1, acc)
    finish(blocks - 1, acc)

    total = hsend[0:LAT, :]
    for j in range(1, ns):
        if not hops(half - j // 2, j % 2):
            straight(j).wait_recv()
            total = total + obuf[j * LAT:(j + 1) * LAT, :].astype(F32)
    mine[...] = latent_t + step_size * total
    pass_on = to_frame(mine, theirs, m_sems.at[0], m_sems.at[1], before)
    pass_on.start()
    vel_ref[0] = total

    rest = pl.ds(TOKS, (ns - 1) * TOKS)
    rest_lat = pl.ds(LAT, (ns - 1) * LAT)
    to_seq(keys.at[rest], keys.at[rest], k_out, k_in.at[0], here).wait_send()
    to_seq(vals.at[rest_lat], vals.at[rest_lat], v_out, v_in.at[0], here).wait_send()
    to_seq(qbuf.at[rest], qbuf.at[rest], q_out, q_in.at[0], here).wait_send()
    for j in range(1, ns):
        if hops(half - j // 2, j % 2):
            step_on(j, j % 2).wait_send()
        else:
            straight(j).wait_send()
    for side in range(2):
        whole = pl.ds(0, toks)
        whole_lat = pl.ds(0, ns * LAT)
        to_frame(keys.at[whole], keys.at[whole], f_out.at[2 * side], f_in.at[0, 0], place).wait_send()
        to_frame(vals.at[whole_lat], vals.at[whole_lat], f_out.at[2 * side + 1], f_in.at[0, 0], place).wait_send()
    pass_on.wait()
    last = jnp.full((LAT, TOKS), place, jnp.int32) == nf - 1
    new_ref[0] = jnp.where(last, noise_ref[...], theirs[...])


def on_device(nf, ns, queries, key_proj, values, back_count, ahead_count, timestep, latent, noise_frame, w_final):
    vmem = pl.BlockSpec(memory_space=pltpu.VMEM)
    anywhere = pl.BlockSpec(memory_space=pltpu.HBM)
    toks = ns * TOKS
    dma = pltpu.SemaphoreType.DMA
    out = jax.ShapeDtypeStruct((1, LAT, TOKS), F32)
    pairs = 2 * toks * 3 * toks
    velocity, new_queue = pl.pallas_call(
        functools.partial(kernel, ns, nf),
        out_shape=(out, out),
        in_specs=[anywhere] * 9,
        out_specs=(vmem, vmem),
        scratch_shapes=[
            pltpu.SMEM((1,), jnp.int32),
            pltpu.SMEM((1,), jnp.int32),
            pltpu.SMEM((1,), jnp.int32),
            pltpu.VMEM((TOKS, ns * HD), BF16),
            pltpu.VMEM((LAT, ns * HD), BF16),
            pltpu.VMEM((LAT, TOKS), F32),
            pltpu.VMEM((LAT, TOKS), F32),
            pltpu.VMEM((3 * toks, HD), BF16),
            pltpu.VMEM((3 * ns * LAT, TOKS), BF16),
            pltpu.VMEM((ns * LAT, TOKS), BF16),
            pltpu.VMEM((LAT + SUMS, 3 * toks), BF16),
            pltpu.VMEM((toks, HD), BF16),
            pltpu.VMEM((ns * LAT, TOKS), BF16),
            pltpu.VMEM((ns * LAT, TOKS), BF16),
            pltpu.VMEM((ns * LAT, TOKS), F32),
            pltpu.VMEM((ns * LAT, TOKS), F32),
            pltpu.VMEM((LAT, TOKS), F32),
            pltpu.VMEM((LAT, TOKS), F32),
            pltpu.VMEM((3 * toks, PAIR), F32),
            pltpu.VMEM((3 * toks, PAIR), F32),
            dma((9,)), dma, dma, dma, dma((ns,)), dma((ns,)), dma((4,)), dma((2,)),
            dma((ns,)), dma((ns,)), dma((ns,)), dma((ns,)), dma((ns,)), dma((4, GROUPS)),
        ],
        compiler_params=pltpu.CompilerParams(
            collective_id=0, has_side_effects=True, vmem_limit_bytes=(64 << 20) - (400 << 10)),
        cost_estimate=pl.CostEstimate(
            flops=pairs * (HD + LAT), bytes_accessed=4 << 20, transcendentals=pairs // 2),
    )(back_count, ahead_count, timestep, queries, key_proj, values,
      w_final.T, jnp.swapaxes(latent, 1, 2), noise_frame.T)
    return jnp.swapaxes(velocity, 1, 2), jnp.swapaxes(new_queue, 1, 2)


def solution(mesh):
    nf, ns = mesh.shape["frame"], mesh.shape["seq"]
    spread = P("frame", "seq", None)
    placed = (spread, spread, spread, P("frame"), P("frame"), P("frame"), spread, P("seq", None), P())
    return jax.shard_map(
        functools.partial(on_device, nf, ns),
        mesh=mesh,
        in_specs=placed,
        out_specs=(spread, spread),
        check_vma=False,
    )
```

profile of v0, /device:TPU:1, one launch (start us, length us, event | category | flops | bytes accessed | tf_op | source)
XLA Modules:
  0.0 95.0 jit_solution(7510140279510749710)
XLA Ops:
  2.6 90.4 %shard_map.104 = (f32[1,64,128]{2,1,0:T(8,128)}, f32[1,64,128]{2,1,0:T(8,128)}) custom-call(s32[1]{0:T(128)S(6)} %copy.13.back_hbm, s32[1]{0:T(128)S(6)} %copy.14.ahead_hbm, s32[1]{0:T(128)S(6)} %copy.15.time_hbm, bf16[1,128,2048]{2,1,0:T(8,128)(2,1)} %q_hbm.1, bf16[1,128,2048]{2,1,0:T(8,128)(2,1)} %k_hbm.1, bf16[1,128,2048]{2,1,0:T(8,128)(2,1)} %v_hbm.1, ...), custom_call_target="tpu_custom_call" | custom-call | flops 4831838208 | bytes 4194304 | tf_op jit(solution)/shard_map/pallas_call | solution.py:312
  93.0 0.0 copy-start
  93.0 1.4 %copy.16 = f32[1,128,64]{1,2,0:T(8,128)} copy(f32[1,128,64]{1,2,0:T(8,128)} %bitcast.6) | data formatting | bytes 65536
  94.3 0.0 copy-done
  94.3 0.6 copy.17
Async XLA Ops:
  93.0 1.4 %copy-start = (f32[1,64,128]{2,1,0:T(8,128)S(1)}, f32[1,64,128]{2,1,0:T(8,128)}, u32[]{:S(2)}) copy-start(f32[1,64,128]{2,1,0:T(8,128)} %get-tuple-element.5) | copy-start | bytes 98308
where the time goes:
time: 95.2 us; the launch traced here: 95 us
  Pallas kernels  90.4 us (95%)
  between operations  2.58 us (3%)
  local copies, waits for them, and re-layouts  2 us (2%)
    pallas_call x1, Pallas kernels, on_device(): pl.pallas_call(functools.partial(kernel, ns, nf), out_shape=(out, out), i...  90.4 us
    unnamed x4, local copies, waits for them, and re-layouts  2 us

commit v1 on v0

--- a/solution.py
+++ b/solution.py
@@ -19,7 +19,6 @@
 PAIR = 2 * TOKS
 SUMS = 16
 GROUPS = 4
-HOPS = ()
 
 
 def sigma_of(index):
@@ -28,10 +27,11 @@
 
 
 def kernel(
-    ns, nf, back_hbm, ahead_hbm, time_hbm, q_hbm, k_hbm, v_hbm, w_hbm, latent_hbm, noise_hbm,
-    vel_ref, new_ref,
-    back_ref, ahead_ref, time_ref, v_ref, w_ref, latent_ref, noise_ref, keys, vals, vsend, weighted, qbuf, osend, obuf, hsend, hbuf, mine, theirs, s0, s1,
-    own_sem, k_out, v_out, q_out, o_out, h_out, f_out, m_sems, k_in, v_in, q_in, o_in, h_in, f_in,
+    ns, nf, back_hbm, ahead_hbm, time_hbm, q_hbm, k_hbm, v_hbm, w_hbm, latent_hbm,
+    vel_hbm, new_hbm,
+    back_ref, ahead_ref, time_ref, v_ref, w_ref, latent_ref, vel_ref,
+    keys, vals, vsend, weighted, qbuf, osend, obuf, own, mine, s0, s1,
+    own_sem, k_out, v_out, q_out, o_out, f_out, m_sems, k_in, v_in, q_in, o_in, f_in,
 ):
     place, here = lax.axis_index("frame"), lax.axis_index("seq")
     after, before = lax.rem(place + 1, nf), lax.rem(place + nf - 1, nf)
@@ -42,8 +42,11 @@
     def offset(j):
         return jnp.where(j == 0, 0, jnp.where(j % 2 == 0, half - j // 2, (j - 1) // 2 - half))
 
-    def peer(j, sign):
-        return lax.rem(here + sign * offset(j) + ns, ns)
+    def ring(z):
+        return lax.rem(z + ns, ns)
+
+    def owner(j):
+        return ring(here - offset(j))
 
     def rows(j, count=1):
         return pl.ds(pl.multiple_of(j * TOKS, TOKS), count * TOKS)
@@ -64,7 +67,7 @@
     barrier = pltpu.get_barrier_semaphore()
 
     def greet(j, _):
-        pl.semaphore_signal(barrier, inc=1, device_id={"seq": peer(j, 1)},
+        pl.semaphore_signal(barrier, inc=1, device_id={"seq": ring(here + j)},
                             device_id_type=pl.DeviceIdType.MESH)
         return 0
 
@@ -79,30 +82,30 @@
     own_v = pltpu.make_async_copy(v_hbm.at[0], v_ref, own_sem.at[2])
     own_w = pltpu.make_async_copy(w_hbm, w_ref, own_sem.at[3])
     own_latent = pltpu.make_async_copy(latent_hbm.at[0], latent_ref, own_sem.at[4])
-    own_noise = pltpu.make_async_copy(noise_hbm, noise_ref, own_sem.at[5])
+    out_vel = pltpu.make_async_copy(vel_ref, vel_hbm.at[0], own_sem.at[5])
     scalars = [
         pltpu.make_async_copy(src, dst, own_sem.at[6 + i])
         for i, (src, dst) in enumerate(((back_hbm, back_ref), (ahead_hbm, ahead_ref), (time_hbm, time_ref)))
     ]
     own_q = pltpu.make_async_copy(q_hbm.at[0, :, columns(here)], qbuf.at[rows(0)], own_sem.at[0])
     own_k = pltpu.make_async_copy(k_hbm.at[0, :, columns(here)], keys.at[rows(0)], own_sem.at[1])
-    for copy in (own_v, own_w, own_k, own_q, own_latent, own_noise, *scalars):
+    for copy in (own_v, own_w, own_k, own_q, own_latent, *scalars):
         copy.start()
 
     pl.semaphore_wait(barrier, ns + 1)
 
     def send_k(j, _):
-        z = peer(j, 1)
+        z = ring(here + offset(j))
         to_seq(k_hbm.at[0, :, columns(z)], keys.at[rows(j)], k_out, k_in.at[j], z).start()
         return 0
 
     def send_v(j, _):
-        z = peer(j, 1)
+        z = ring(here + offset(j))
         to_seq(vsend.at[lats(z)], vals.at[lats(j)], v_out, v_in.at[j], z).start()
         return 0
 
     def send_q(j, _):
-        z = peer(j, 1)
+        z = ring(here + offset(j))
         to_seq(q_hbm.at[0, :, columns(z)], qbuf.at[rows(j)], q_out, q_in.at[j], z).start()
         return 0
 
@@ -122,7 +125,6 @@
     own_k.wait()
     own_q.wait()
     own_latent.wait()
-    own_noise.wait()
     for copy in scalars:
         copy.wait()
 
@@ -177,12 +179,6 @@
     chunks = 3 * toks // CHUNK
     blocks = ns // 2
 
-    def hops(d, i):
-        return d in HOPS and d <= half - 1 + i
-
-    def gets(d, i):
-        return hops(d + 1, i)
-
     def wait_q(b):
         for j in (2 * b, 2 * b + 1):
             if not isinstance(j, int) or j > 0:
@@ -201,47 +197,23 @@
         r = jnp.dot(weighted[:, c * CHUNK:(c + 1) * CHUNK], p, preferred_element_type=F32)
         return r if acc is None else acc + r
 
-    def step_on(j, i):
-        z = lax.rem(here + (1 if i else ns - 1), ns)
-        return to_seq(hsend.at[lats(j)], hbuf.at[lats(j + 2)], h_out.at[j], h_in.at[j + 2], z)
-
     def straight(j):
-        return to_seq(osend.at[lats(j)], obuf.at[lats(j)], o_out.at[j], o_in.at[j], peer(j, -1))
+        return to_seq(osend.at[lats(j)], obuf.at[lats(j)], o_out.at[j], o_in.at[j], owner(j))
 
     def finish(b, acc):
         out = acc[0:LAT] / acc[LAT:LAT + 1]
         for i in range(2):
             j = 2 * b + i
-            mine_now = out[:, i * TOKS:(i + 1) * TOKS]
-            if isinstance(b, int):
-                if gets(half - b, i):
-                    step_on(j - 2, i).wait_recv()
-                    mine_now = mine_now + hbuf[lats(j), :]
-                if hops(half - b, i):
-                    hsend[lats(j), :] = mine_now
-                    step_on(j, i).start()
-                else:
-                    osend[lats(j), :] = mine_now.astype(BF16)
-                    straight(j).start()
-            else:
-                given, stepped, own = (
-                    functools.reduce(jnp.logical_or, [b == half - d for d in range(1, half + 1) if test(d, i)], False)
-                    for test in (gets, hops, lambda d, i: d == half and i == 0))
-                hsend[lats(j), :] = mine_now
-
-                @pl.when(given)
+            part = out[:, i * TOKS:(i + 1) * TOKS]
+            osend[lats(j), :] = part.astype(BF16)
+            if i == 0:
+                @pl.when(j == 0)
                 def _():
-                    step_on(j - 2, i).wait_recv()
-                    hsend[lats(j), :] = hsend[lats(j), :] + hbuf[lats(j), :]
-
-                @pl.when(stepped)
-                def _():
-                    step_on(j, i).start()
-
-                @pl.when(jnp.logical_not(jnp.logical_or(stepped, own)))
-                def _():
-                    osend[lats(j), :] = hsend[lats(j), :].astype(BF16)
-                    straight(j).start()
+                    own[...] = part
+
+            @pl.when(j > 0)
+            def _():
+                straight(j).start()
 
     def peak(top):
         return jnp.max(top, axis=0, keepdims=True) * RATE
@@ -272,15 +244,15 @@
         acc = gather(m, c, s1, acc)
     finish(blocks - 1, acc)
 
-    total = hsend[0:LAT, :]
+    total = own[...]
     for j in range(1, ns):
-        if not hops(half - j // 2, j % 2):
-            straight(j).wait_recv()
-            total = total + obuf[j * LAT:(j + 1) * LAT, :].astype(F32)
+        to_seq(obuf.at[lats(j)], obuf.at[lats(j)], o_out.at[j], o_in.at[j], here).wait_recv()
+        total = total + obuf[j * LAT:(j + 1) * LAT, :].astype(F32)
     mine[...] = latent_t + step_size * total
-    pass_on = to_frame(mine, theirs, m_sems.at[0], m_sems.at[1], before)
+    pass_on = to_frame(mine, new_hbm.at[0], m_sems.at[0], m_sems.at[1], before)
     pass_on.start()
-    vel_ref[0] = total
+    vel_ref[...] = total
+    out_vel.start()
 
     rest = pl.ds(TOKS, (ns - 1) * TOKS)
     rest_lat = pl.ds(LAT, (ns - 1) * LAT)
@@ -288,32 +260,33 @@
     to_seq(vals.at[rest_lat], vals.at[rest_lat], v_out, v_in.at[0], here).wait_send()
     to_seq(qbuf.at[rest], qbuf.at[rest], q_out, q_in.at[0], here).wait_send()
     for j in range(1, ns):
-        if hops(half - j // 2, j % 2):
-            step_on(j, j % 2).wait_send()
-        else:
-            straight(j).wait_send()
+        to_seq(osend.at[lats(j)], osend.at[lats(j)], o_out.at[j], o_in.at[j], here).wait_send()
     for side in range(2):
         whole = pl.ds(0, toks)
         whole_lat = pl.ds(0, ns * LAT)
         to_frame(keys.at[whole], keys.at[whole], f_out.at[2 * side], f_in.at[0, 0], place).wait_send()
         to_frame(vals.at[whole_lat], vals.at[whole_lat], f_out.at[2 * side + 1], f_in.at[0, 0], place).wait_send()
     pass_on.wait()
-    last = jnp.full((LAT, TOKS), place, jnp.int32) == nf - 1
-    new_ref[0] = jnp.where(last, noise_ref[...], theirs[...])
+    out_vel.wait()
+
+
+def closing(nf, vel_ref, arrived_ref, noise_ref, vel_out, new_out):
+    last = jnp.full((LAT, TOKS), lax.axis_index("frame"), jnp.int32) == nf - 1
+    vel_out[...] = vel_ref[...]
+    new_out[0] = jnp.where(last, noise_ref[...], arrived_ref[0])
 
 
 def on_device(nf, ns, queries, key_proj, values, back_count, ahead_count, timestep, latent, noise_frame, w_final):
-    vmem = pl.BlockSpec(memory_space=pltpu.VMEM)
     anywhere = pl.BlockSpec(memory_space=pltpu.HBM)
     toks = ns * TOKS
     dma = pltpu.SemaphoreType.DMA
     out = jax.ShapeDtypeStruct((1, LAT, TOKS), F32)
     pairs = 2 * toks * 3 * toks
-    velocity, new_queue = pl.pallas_call(
+    velocity, arrived = pl.pallas_call(
         functools.partial(kernel, ns, nf),
         out_shape=(out, out),
-        in_specs=[anywhere] * 9,
-        out_specs=(vmem, vmem),
+        in_specs=[anywhere] * 8,
+        out_specs=(anywhere, anywhere),
         scratch_shapes=[
             pltpu.SMEM((1,), jnp.int32),
             pltpu.SMEM((1,), jnp.int32),
@@ -329,21 +302,25 @@
             pltpu.VMEM((toks, HD), BF16),
             pltpu.VMEM((ns * LAT, TOKS), BF16),
             pltpu.VMEM((ns * LAT, TOKS), BF16),
-            pltpu.VMEM((ns * LAT, TOKS), F32),
-            pltpu.VMEM((ns * LAT, TOKS), F32),
             pltpu.VMEM((LAT, TOKS), F32),
             pltpu.VMEM((LAT, TOKS), F32),
             pltpu.VMEM((3 * toks, PAIR), F32),
             pltpu.VMEM((3 * toks, PAIR), F32),
-            dma((9,)), dma, dma, dma, dma((ns,)), dma((ns,)), dma((4,)), dma((2,)),
-            dma((ns,)), dma((ns,)), dma((ns,)), dma((ns,)), dma((ns,)), dma((4, GROUPS)),
+            dma((9,)), dma, dma, dma, dma((ns,)), dma((4,)), dma((2,)),
+            dma((ns,)), dma((ns,)), dma((ns,)), dma((ns,)), dma((4, GROUPS)),
         ],
         compiler_params=pltpu.CompilerParams(
             collective_id=0, has_side_effects=True, vmem_limit_bytes=(64 << 20) - (400 << 10)),
         cost_estimate=pl.CostEstimate(
             flops=pairs * (HD + LAT), bytes_accessed=4 << 20, transcendentals=pairs // 2),
     )(back_count, ahead_count, timestep, queries, key_proj, values,
-      w_final.T, jnp.swapaxes(latent, 1, 2), noise_frame.T)
+      w_final.T, jnp.swapaxes(latent, 1, 2))
+    velocity, new_queue = pl.pallas_call(
+        functools.partial(closing, nf),
+        out_shape=(out, out),
+        in_specs=[pl.BlockSpec(memory_space=pltpu.VMEM)] * 3,
+        out_specs=(pl.BlockSpec(memory_space=pltpu.VMEM),) * 2,
+    )(velocity, arrived, noise_frame.T)
     return jnp.swapaxes(velocity, 1, 2), jnp.swapaxes(new_queue, 1, 2)
 
 

time: 95.2 us -> 93.8 us (0.985)
  local copies, waits for them, and re-layouts: 2 us -> 0 us
    unnamed x4 -> x0, local copies, waits for them, and re-layouts: 2 us -> none
    pallas_call x0 -> x1, Pallas kernels: none -> 1.42 us  [on_device(): pl.pallas_call(functools.partial(closing, nf), out_shape=(out, out), in_s...]
where the time goes in v1:
time: 93.8 us; the launch traced here: 93.6 us
  Pallas kernels  91 us (97%)
  between operations  2.58 us (3%)
    pallas_call x1, Pallas kernels, on_device(): pl.pallas_call(functools.partial(kernel, ns, nf), out_shape=(out, out), i...  89.6 us

profile of v1, /device:TPU:1, one launch (start us, length us, event | category | flops | bytes accessed | tf_op | source)
XLA Modules:
  0.0 93.6 jit_solution(8842669533114847173)
XLA Ops:
  2.6 89.6 %shard_map.104 = (f32[1,64,128]{2,1,0:T(8,128)}, f32[1,64,128]{2,1,0:T(8,128)}) custom-call(s32[1]{0:T(128)S(6)} %copy.11.back_hbm, s32[1]{0:T(128)S(6)} %copy.12.ahead_hbm, s32[1]{0:T(128)S(6)} %copy.13.time_hbm, bf16[1,128,2048]{2,1,0:T(8,128)(2,1)} %q_hbm.1, bf16[1,128,2048]{2,1,0:T(8,128)(2,1)} %k_hbm.1, bf16[1,128,2048]{2,1,0:T(8,128)(2,1)} %v_hbm.1, ...), custom_call_target="tpu_custom_call" | custom-call | flops 4831838208 | bytes 4194304 | tf_op jit(solution)/shard_map/pallas_call | solution.py:285
  92.1 1.4 %shard_map.105 = (f32[1,64,128]{2,1,0:T(8,128)}, f32[1,64,128]{2,1,0:T(8,128)}) custom-call(f32[1,64,128]{2,1,0:T(8,128)} %get-tuple-element.6.vel_ref, f32[1,64,128]{2,1,0:T(8,128)} %get-tuple-element.7.arrived_ref, f32[64,128]{1,0:T(8,128)} %bitcast.5), custom_call_target="tpu_custom_call" | custom-call | tf_op jit(solution)/shard_map/pallas_call | solution.py:318

commit v2 on v1

--- a/solution.py
+++ b/solution.py
@@ -118,8 +118,12 @@
         vsend[h * LAT:(h + 1) * LAT, :] = part.astype(BF16)
 
     lax.fori_loop(1, per, send_v, 0)
-    lax.fori_loop(per, ns, send_k, 0)
-    lax.fori_loop(per, ns, send_v, 0)
+    def send_kv(j, _):
+        send_k(j, 0)
+        send_v(j, 0)
+        return 0
+
+    lax.fori_loop(per, ns, send_kv, 0)
     lax.fori_loop(1, ns, send_q, 0)
     vals[0:LAT, :] = vsend[lats(here), :]
     own_k.wait()

time: 93.8 us -> 93.8 us (level)
  no operation moved by 1% of the time
where the time goes in v2:
time: 93.8 us; the launch traced here: 93.6 us
  Pallas kernels  91 us (97%)
  between operations  2.58 us (3%)
    pallas_call x1, Pallas kernels, on_device(): pl.pallas_call(functools.partial(kernel, ns, nf), out_shape=(out, out), i...  89.6 us

profile of v2, /device:TPU:1, one launch (start us, length us, event | category | flops | bytes accessed | tf_op | source)
XLA Modules:
  0.0 93.6 jit_solution(9208699249015829619)
XLA Ops:
  2.6 89.6 %shard_map.104 = (f32[1,64,128]{2,1,0:T(8,128)}, f32[1,64,128]{2,1,0:T(8,128)}) custom-call(s32[1]{0:T(128)S(6)} %copy.11.back_hbm, s32[1]{0:T(128)S(6)} %copy.12.ahead_hbm, s32[1]{0:T(128)S(6)} %copy.13.time_hbm, bf16[1,128,2048]{2,1,0:T(8,128)(2,1)} %q_hbm.1, bf16[1,128,2048]{2,1,0:T(8,128)(2,1)} %k_hbm.1, bf16[1,128,2048]{2,1,0:T(8,128)(2,1)} %v_hbm.1, ...), custom_call_target="tpu_custom_call" | custom-call | flops 4831838208 | bytes 4194304 | tf_op jit(solution)/shard_map/pallas_call | solution.py:289
  92.2 1.4 %shard_map.105 = (f32[1,64,128]{2,1,0:T(8,128)}, f32[1,64,128]{2,1,0:T(8,128)}) custom-call(f32[1,64,128]{2,1,0:T(8,128)} %get-tuple-element.6.vel_ref, f32[1,64,128]{2,1,0:T(8,128)} %get-tuple-element.7.arrived_ref, f32[64,128]{1,0:T(8,128)} %bitcast.5), custom_call_target="tpu_custom_call" | custom-call | tf_op jit(solution)/shard_map/pallas_call | solution.py:322
